TPU v7x, 32 devices: a whole 2x2x4 slice. The times are simulated.
32 devices in a mesh: row: 4 (over y, x), col: 8 (over z, core).
Axes of the slice: x: 2, y: 2, z: 4, core: 2. Of those that a mesh axis runs over, the one named last changes fastest.
Arguments:
- tokens_b: bfloat16 [512, 12288], P('col', 'row'), may hold values from -6 to 6
- tokens_a: bfloat16 [512, 12288], P('col', 'row'), may hold values from -6 to 6
- upstream_a: bfloat16 [512, 12288], P('col', 'row'), may hold values from -1.5 to 1.5
- up_weight: bfloat16 [12288, 24576], P('row', 'col'), may hold values from -0.0546875 to 0.0546875
- down_weight: bfloat16 [24576, 12288], P('col', 'row'), may hold values from -0.0390625 to 0.0390625
Outputs:
- output_b: bfloat16 [512, 12288], P('col', 'row')
- input_grad: bfloat16 [512, 12288], P('col', 'row')
- up_grad: bfloat16 [12288, 24576], P('row', 'col')
- down_grad: bfloat16 [24576, 12288], P('col', 'row')
All inputs are finite; a program needn't handle non-finite values.
Results may differ from a plain program's by a relative error of at most 0.02.
Values may be sent and summed in bfloat16 or wider, within the bound.
A program may use at most 192 MiB of HBM per device.

v0:
```python
import jax
import jax.numpy as jnp
from jax import lax
from jax.sharding import PartitionSpec as P


def smooth_gate(value):
    return jax.nn.gelu(value, approximate=True)


def activate(hidden_b, hidden_a, grad_gate):
    gated_b = smooth_gate(hidden_b).astype(jnp.bfloat16)
    gated_full, pullback = jax.vjp(smooth_gate, hidden_a)
    grad_pre = pullback(grad_gate)[0].astype(jnp.bfloat16)
    return (gated_b, gated_full.astype(jnp.bfloat16), grad_pre)


def on_device(tokens_b, tokens_a, upstream_a, up_weight, down_weight):
    inputs_b, inputs_a, upstream = (
        lax.all_gather(tokens_b, "col", axis=0, tiled=True),
        lax.all_gather(tokens_a, "col", axis=0, tiled=True),
        lax.all_gather(upstream_a, "col", axis=0, tiled=True),
    )
    partial_b = jnp.dot(inputs_b, up_weight, preferred_element_type=jnp.float32)
    partial_a = jnp.dot(inputs_a, up_weight, preferred_element_type=jnp.float32)
    partial_grad = lax.dot_general(
        upstream, down_weight, (((1,), (1,)), ((), ())), preferred_element_type=jnp.float32
    )
    hidden_b, hidden_a, grad_gate = (
        lax.psum_scatter(
            partial_b.astype(jnp.bfloat16), "row", scatter_dimension=0, tiled=True
        ).astype(jnp.float32),
        lax.psum_scatter(
            partial_a.astype(jnp.bfloat16), "row", scatter_dimension=0, tiled=True
        ).astype(jnp.float32),
        lax.psum_scatter(
            partial_grad.astype(jnp.bfloat16), "row", scatter_dimension=0, tiled=True
        ).astype(jnp.float32),
    )
    share_b, share_a, share_grad = activate(hidden_b, hidden_a, grad_gate)
    gated_b, gated_a, grad_pre = (
        lax.all_gather(share_b, "row", axis=0, tiled=True),
        lax.all_gather(share_a, "row", axis=0, tiled=True),
        lax.all_gather(share_grad, "row", axis=0, tiled=True),
    )
    output_part = jnp.dot(gated_b, down_weight, preferred_element_type=jnp.float32)
    input_part = lax.dot_general(
        grad_pre, up_weight, (((1,), (1,)), ((), ())), preferred_element_type=jnp.float32
    )
    output_b, input_grad = (
        lax.psum_scatter(
            output_part.astype(jnp.bfloat16), "col", scatter_dimension=0, tiled=True
        ).astype(jnp.float32),
        lax.psum_scatter(
            input_part.astype(jnp.bfloat16), "col", scatter_dimension=0, tiled=True
        ).astype(jnp.float32),
    )
    up_grad = lax.dot_general(
        inputs_a, grad_pre, (((0,), (0,)), ((), ())), preferred_element_type=jnp.float32
    )
    down_grad = lax.dot_general(
        gated_a, upstream, (((0,), (0,)), ((), ())), preferred_element_type=jnp.float32
    )
    return (
        output_b.astype(jnp.bfloat16),
        input_grad.astype(jnp.bfloat16),
        up_grad.astype(jnp.bfloat16),
        down_grad.astype(jnp.bfloat16),
    )


def solution(mesh):
    placed = (P("col", "row"), P("col", "row"), P("col", "row"), P("row", "col"), P("col", "row"))
    return jax.shard_map(
        on_device,
        mesh=mesh,
        in_specs=placed,
        out_specs=(P("col", "row"), P("col", "row"), P("row", "col"), P("col", "row")),
        check_vma=False,
    )
```

profile of v0, /device:TPU:29, one launch (start us, length us, event | category | flops | bytes accessed | tf_op | source)
XLA Modules:
  0.0 496.4 jit_solution(2788669460172409957)
XLA Ops:
  7.2 0.0 all-gather.7.cloned.1.call-start
  7.2 0.7 all-gather.7.cloned.1.call-update
  7.9 0.0 all-gather.11.cloned.1.call-start
  7.9 0.7 all-gather.11.cloned.1.call-update
  8.6 0.0 all-gather.13.cloned.1.call-start
  8.7 0.7 all-gather.13.cloned.1.call-update
  9.4 0.0 reduce-scatter.6.cloned.1.call-start
  9.4 37.8 %all-gather.7.cloned.1.call-done = bf16[512,3072]{1,0:T(8,128)(2,1)} async-done(((bf16[64,3072]{1,0:T(8,128)(2,1)}), bf16[512,3072]{1,0:T(8,128)(2,1)}) %all-gather.7.cloned.1.call-update) | async-done | bytes 3145744 | tf_op jit(solution)/shard_map/all_gather | solution.py:20
  47.2 15.8 %convolution_convert_fusion.5 = bf16[512,3072]{1,0:T(8,128)(2,1)} fusion(bf16[512,3072]{1,0:T(8,128)(2,1)} %all-gather.7.cloned.1.call-done, bf16[3072,3072]{1,0:T(8,128)(2,1)} %param.8), kind=kOutput, calls=%fused_computation.6 | convolution fusion | flops 9665249280 | bytes 25165824 | tf_op jit(solution)/shard_map/dot_general | solution.py:24
  63.0 0.0 reduce-scatter.6.cloned.1.call-update
  63.0 0.0 reduce-scatter.10.cloned.1.call-start
  63.1 23.0 %all-gather.11.cloned.1.call-done = bf16[512,3072]{1,0:T(8,128)(2,1)} async-done(((bf16[64,3072]{1,0:T(8,128)(2,1)}), bf16[512,3072]{1,0:T(8,128)(2,1)}) %all-gather.11.cloned.1.call-update) | async-done | bytes 3145744 | tf_op jit(solution)/shard_map/all_gather | solution.py:22
  86.0 15.9 %convolution_convert_fusion.3 = bf16[512,3072]{1,0:T(8,128)(2,1)} fusion(bf16[512,3072]{1,0:T(8,128)(2,1)} %all-gather.11.cloned.1.call-done, bf16[3072,3072]{1,0:T(8,128)(2,1)} %param.9), kind=kOutput, calls=%fused_computation.4 | convolution fusion | flops 9665249280 | bytes 25165824 | tf_op jit(solution)/shard_map/dot_general | solution.py:26
  101.9 0.0 reduce-scatter.10.cloned.1.call-update
  101.9 0.0 reduce-scatter.12.cloned.1.call-start
  102.0 22.9 %all-gather.13.cloned.1.call-done = bf16[512,3072]{1,0:T(8,128)(2,1)} async-done(((bf16[64,3072]{1,0:T(8,128)(2,1)}), bf16[512,3072]{1,0:T(8,128)(2,1)}) %all-gather.13.cloned.1.call-update) | async-done | bytes 3145744 | tf_op jit(solution)/shard_map/all_gather | solution.py:21
  124.9 15.8 %convolution_convert_fusion.2 = bf16[512,3072]{1,0:T(8,128)(2,1)} fusion(bf16[512,3072]{1,0:T(8,128)(2,1)} %all-gather.13.cloned.1.call-done, bf16[3072,3072]{1,0:T(8,128)(2,1)} %param.8), kind=kOutput, calls=%fused_computation.3 | convolution fusion | flops 9665249280 | bytes 25165824 | tf_op jit(solution)/shard_map/dot_general | solution.py:25
  140.7 0.0 reduce-scatter.12.cloned.1.call-update
  140.7 0.0 all-gather.9.cloned.1.call-start
  140.7 32.0 %reduce-scatter.6.cloned.1.call-done = bf16[128,3072]{1,0:T(8,128)(2,1)} async-done(((bf16[512,3072]{1,0:T(8,128)(2,1)}), bf16[128,3072]{1,0:T(8,128)(2,1)}) %reduce-scatter.6.cloned.1.call-update) | async-done | bytes 786448 | tf_op jit(solution)/shard_map/reduce_scatter | solution.py:30
  172.7 2.5 fusion.10
  175.3 0.0 all-gather.9.cloned.1.call-update
  175.3 0.2 all-gather.15.cloned.1.call-start
  175.5 44.0 %reduce-scatter.10.cloned.1.call-done = bf16[128,3072]{1,0:T(8,128)(2,1)} async-done(((bf16[512,3072]{1,0:T(8,128)(2,1)}), bf16[128,3072]{1,0:T(8,128)(2,1)}) %reduce-scatter.10.cloned.1.call-update) | async-done | bytes 786448 | tf_op jit(solution)/shard_map/reduce_scatter | solution.py:36
  219.5 47.4 %reduce-scatter.12.cloned.1.call-done = bf16[128,3072]{1,0:T(8,128)(2,1)} async-done(((bf16[512,3072]{1,0:T(8,128)(2,1)}), bf16[128,3072]{1,0:T(8,128)(2,1)}) %reduce-scatter.12.cloned.1.call-update) | async-done | bytes 786448 | tf_op jit(solution)/shard_map/reduce_scatter | solution.py:33
  266.9 3.7 fusion.16
  270.7 0.0 all-gather.15.cloned.1.call-update
  270.7 0.0 all-gather.17.cloned.1.call-start
  270.7 0.7 all-gather.17.cloned.1.call-update
  271.4 0.0 reduce-scatter.8.cloned.1.call-start
  271.5 41.9 %all-gather.9.cloned.1.call-done = bf16[512,3072]{1,0:T(8,128)(2,1)} async-done(((bf16[128,3072]{1,0:T(8,128)(2,1)}), bf16[512,3072]{1,0:T(8,128)(2,1)}) %all-gather.9.cloned.1.call-update) | async-done | bytes 3145744 | tf_op jit(solution)/shard_map/all_gather | solution.py:42
  313.4 15.9 %convolution_convert_fusion.4 = bf16[512,3072]{1,0:T(8,128)(2,1)} fusion(bf16[512,3072]{1,0:T(8,128)(2,1)} %all-gather.9.cloned.1.call-done, bf16[3072,3072]{1,0:T(8,128)(2,1)} %param.9), kind=kOutput, calls=%fused_computation.5 | convolution fusion | flops 9665249280 | bytes 25165824 | tf_op jit(solution)/shard_map/dot_general | solution.py:46
  329.3 0.0 reduce-scatter.8.cloned.1.call-update
  329.3 0.0 reduce-scatter.14.cloned.1.call-start
  329.3 30.5 %all-gather.15.cloned.1.call-done = bf16[512,3072]{1,0:T(8,128)(2,1)} async-done(((bf16[128,3072]{1,0:T(8,128)(2,1)}), bf16[512,3072]{1,0:T(8,128)(2,1)}) %all-gather.15.cloned.1.call-update) | async-done | bytes 3145744 | tf_op jit(solution)/shard_map/all_gather | solution.py:44
  359.8 15.9 %convolution_convert_fusion.1 = bf16[512,3072]{1,0:T(8,128)(2,1)} fusion(bf16[512,3072]{1,0:T(8,128)(2,1)} %all-gather.15.cloned.1.call-done, bf16[3072,3072]{1,0:T(8,128)(2,1)} %param.8), kind=kOutput, calls=%fused_computation.2 | convolution fusion | flops 9665249280 | bytes 25165824 | tf_op jit(solution)/shard_map/dot_general | solution.py:47
  375.8 0.0 copy-start.1
  375.8 0.0 reduce-scatter.14.cloned.1.call-update
  375.8 1.9 copy-done.1
  377.7 15.0 %convert_bitcast_fusion = bf16[3072,3072]{0,1:T(8,128)(2,1)} fusion(bf16[512,3072]{1,0:T(8,128)(2,1)} %all-gather.15.cloned.1.call-done, bf16[512,3072]{1,0:T(8,128)(2,1)S(1)} %copy-done.1), kind=kOutput, calls=%fused_computation | convolution fusion | flops 9673113600 | bytes 25165824 | tf_op jit(solution)/shard_map/dot_general | solution.py:58
  392.7 0.0 copy-start
  392.7 24.7 %copy.9 = bf16[3072,3072]{1,0:T(8,128)(2,1)} copy(bf16[3072,3072]{0,1:T(8,128)(2,1)} %convert_bitcast_fusion) | data formatting | bytes 37748736
  417.4 0.0 all-gather.17.cloned.1.call-done
  417.4 0.0 copy-done
  417.4 15.1 %convolution_convert_fusion = bf16[3072,3072]{1,0:T(8,128)(2,1)} fusion(bf16[512,3072]{1,0:T(8,128)(2,1)} %all-gather.17.cloned.1.call-done, bf16[512,3072]{1,0:T(8,128)(2,1)S(1)} %copy-done), kind=kOutput, calls=%fused_computation.1 | convolution fusion | flops 9673113600 | bytes 25165824 | tf_op jit(solution)/shard_map/dot_general | solution.py:61
  432.5 14.9 %reduce-scatter.8.cloned.1.call-done = bf16[64,3072]{1,0:T(8,128)(2,1)} async-done(((bf16[512,3072]{1,0:T(8,128)(2,1)}), bf16[64,3072]{1,0:T(8,128)(2,1)}) %reduce-scatter.8.cloned.1.call-update) | async-done | bytes 393232 | tf_op jit(solution)/shard_map/reduce_scatter | solution.py:51
  447.5 42.4 %reduce-scatter.14.cloned.1.call-done = bf16[64,3072]{1,0:T(8,128)(2,1)} async-done(((bf16[512,3072]{1,0:T(8,128)(2,1)}), bf16[64,3072]{1,0:T(8,128)(2,1)}) %reduce-scatter.14.cloned.1.call-update) | async-done | bytes 393232 | tf_op jit(solution)/shard_map/reduce_scatter | solution.py:54
Async XLA Ops:
  7.2 40.1 %all-gather.7.cloned.1.call-start = ((), (), s32[]{:S(2)}) async-start(), calls=%async_computation.5 | async-start | bytes 3538944 | tf_op jit(solution)/shard_map/all_gather | solution.py:20
  7.9 78.1 %all-gather.11.cloned.1.call-start = ((), (), s32[]{:S(2)}) async-start(), calls=%async_computation.9 | async-start | bytes 3538944 | tf_op jit(solution)/shard_map/all_gather | solution.py:22
  8.6 116.2 %all-gather.13.cloned.1.call-start = ((), (), s32[]{:S(2)}) async-start(), calls=%async_computation.11 | async-start | bytes 3538944 | tf_op jit(solution)/shard_map/all_gather | solution.py:21
  9.4 163.4 %reduce-scatter.6.cloned.1.call-start = ((), (), s32[]{:S(2)}) async-start(), calls=%async_computation.6 | async-start | bytes 3932160 | tf_op jit(solution)/shard_map/reduce_scatter | solution.py:30
  63.0 156.5 %reduce-scatter.10.cloned.1.call-start = ((), (), s32[]{:S(2)}) async-start(), calls=%async_computation.10 | async-start | bytes 3932160 | tf_op jit(solution)/shard_map/reduce_scatter | solution.py:36
  101.9 165.0 %reduce-scatter.12.cloned.1.call-start = ((), (), s32[]{:S(2)}) async-start(), calls=%async_computation.12 | async-start | bytes 3932160 | tf_op jit(solution)/shard_map/reduce_scatter | solution.py:33
  140.7 172.7 %all-gather.9.cloned.1.call-start = ((), (), s32[]{:S(2)}) async-start(), calls=%async_computation.7 | async-start | bytes 3932160 | tf_op jit(solution)/shard_map/all_gather | solution.py:42
  175.3 184.5 %all-gather.15.cloned.1.call-start = ((), (), s32[]{:S(2)}) async-start(), calls=%async_computation.13 | async-start | bytes 3932160 | tf_op jit(solution)/shard_map/all_gather | solution.py:44
  270.7 146.8 %all-gather.17.cloned.1.call-start = ((), (), s32[]{:S(2)}) async-start(), calls=%async_computation.15 | async-start | bytes 3932160 | tf_op jit(solution)/shard_map/all_gather | solution.py:43
  271.4 176.1 %reduce-scatter.8.cloned.1.call-start = ((), (), s32[]{:S(2)}) async-start(), calls=%async_computation.8 | async-start | bytes 3538944 | tf_op jit(solution)/shard_map/reduce_scatter | solution.py:51
  329.3 160.6 %reduce-scatter.14.cloned.1.call-start = ((), (), s32[]{:S(2)}) async-start(), calls=%async_computation.14 | async-start | bytes 3538944 | tf_op jit(solution)/shard_map/reduce_scatter | solution.py:54
  375.8 1.9 copy-start.1
  392.7 24.7 %copy-start = (bf16[512,3072]{1,0:T(8,128)(2,1)S(1)}, bf16[512,3072]{1,0:T(8,128)(2,1)}, u32[]{:S(2)}) copy-start(bf16[512,3072]{1,0:T(8,128)(2,1)} %all-gather.11.cloned.1.call-done) | copy-start | bytes 9437188
Sparse Core Ops, SparseCore 0:
  9.6 37.5 all-gather.6
  48.9 37.1 all-gather.10
  87.7 37.1 all-gather.12
  128.3 44.4 reduce-scatter.5
  175.6 43.9 reduce-scatter.9
  223.0 43.9 reduce-scatter.11
  269.3 44.0 all-gather.8
  315.8 43.9 all-gather.14
  361.7 43.9 all-gather.16
  408.4 39.0 reduce-scatter.7
  450.4 39.4 reduce-scatter.13
where the time goes:
time: 500 us; the launch traced here: 496 us
  waiting for transfers between devices  340 us (68%)
  matrix products  109 us (22%)
  local copies, waits for them, and re-layouts  26.6 us (5%)
  between operations  13.9 us (3%)
  other arithmetic  6.29 us (1%)
    reduce_scatter x1, waiting for transfers between devices, on_device(): lax.psum_scatter(partial_a.astype(jnp.bfloat16), 'row', scatter_dimension...  47.4 us
    reduce_scatter x1, waiting for transfers between devices, on_device(): lax.psum_scatter(partial_grad.astype(jnp.bfloat16), 'row', scatter_dimens...  44 us
    reduce_scatter x1, waiting for transfers between devices, on_device(): lax.psum_scatter(input_part.astype(jnp.bfloat16), 'col', scatter_dimensio...  42.4 us
    all_gather x1, waiting for transfers between devices, on_device(): lax.all_gather(share_b, 'row', axis=0, tiled=True)  41.9 us
    all_gather x1, waiting for transfers between devices, on_device(): lax.all_gather(tokens_b, 'col', axis=0, tiled=True)  37.8 us
    reduce_scatter x1, waiting for transfers between devices, on_device(): lax.psum_scatter(partial_b.astype(jnp.bfloat16), 'row', scatter_dimension...  32 us
    all_gather x1, waiting for transfers between devices, on_device(): lax.all_gather(share_grad, 'row', axis=0, tiled=True)  30.5 us
    unnamed x5, local copies, waits for them, and re-layouts  26.6 us
  transfers between devices with their start and end apart: 11, of which 10 were waited for; matrix products, arithmetic and copies ran while one was open for 28% of the time, Pallas kernels for 0%

commit v1 on v0

v1 whole, which is shorter than its diff:
```python
import functools

import jax
import jax.numpy as jnp
from jax import lax
from jax.experimental import pallas as pl
from jax.experimental.pallas import tpu as pltpu
from jax.sharding import PartitionSpec as P

BF = jnp.bfloat16
F32 = jnp.float32
MESH = pl.DeviceIdType.MESH
SCALE = 0.7978845608028654
CUBIC = 0.044715


def gelu(v):
    return 0.5 * v * (1.0 + jnp.tanh(SCALE * (v + CUBIC * (v * v * v))))


def gelu_both(v):
    t = jnp.tanh(SCALE * (v + CUBIC * (v * v * v)))
    half = 0.5 * (1.0 + t)
    slope = half + 0.5 * v * (1.0 - t * t) * (SCALE * (1.0 + (3.0 * CUBIC) * (v * v)))
    return v * half, slope


def kernel(
    nr, nc, chunk, groups,
    tok_b, tok_a, ups, w_up, w_down,
    out_b, in_grad, all_a, all_u, all_ga, all_gp,
    t_buf, p_buf, r_buf, g_buf, o_buf, sib_buf, z_buf, w_col, w_row,
    ag_send, ag_recv, fw_send, fw_recv, rs_send, rs_recv, rg_send, rg_recv,
    sb_send, sb_recv, zs_send, zs_recv, loc_sem, w_sem, out_sem,
):
    nz = nc // 2
    row = lax.axis_index("row")
    col = lax.axis_index("col")
    z, core = col // 2, col % 2
    tb = tok_b.shape[0]
    width = tok_b.shape[1]
    ff = w_up.shape[1]
    tokens = tb * nc
    rb = tokens // nr
    sibling = (row, z * 2 + 1 - core)

    def rpeer(k):
        return lax.rem(row + k, nr)

    def zpeer(k):
        return lax.rem(z + k, nz)

    def rows_of(index, size):
        return pl.ds(pl.multiple_of(index * size, size), size)

    def cols_of(index, size):
        return pl.ds(pl.multiple_of(index * size, 128), size)

    barrier = pltpu.get_barrier_semaphore()
    for k in range(1, nr):
        pl.semaphore_signal(barrier, inc=1, device_id=(rpeer(k), col), device_id_type=MESH)
    for k in range(1, nz):
        pl.semaphore_signal(barrier, inc=1, device_id=(row, zpeer(k) * 2 + core), device_id_type=MESH)
    pl.semaphore_signal(barrier, inc=1, device_id=sibling, device_id_type=MESH)
    pl.semaphore_wait(barrier, nr - 1 + nz)

    def remote(src, dst, send, recv, device):
        return pltpu.make_async_remote_copy(
            src_ref=src, dst_ref=dst, send_sem=send, recv_sem=recv, device_id=device, device_id_type=MESH
        )

    mine = rows_of(col, tb)
    sources = (tok_b, tok_a, ups)
    gather = []
    for s in range(3):
        pltpu.make_async_copy(sources[s], t_buf.at[s, mine, :], loc_sem.at[s]).start()
        one = []
        for k in range(1, nz):
            c = remote(sources[s], t_buf.at[s, mine, :], ag_send.at[s, k], ag_recv.at[s, k],
                       (row, zpeer(k) * 2 + core))
            c.start()
            one.append(c)
        c = remote(sources[s], t_buf.at[s, mine, :], fw_send.at[s, 0], fw_recv.at[s, 0], sibling)
        c.start()
        gather.append((one, c))

    forwards = []

    def arrive(s):
        mine_now = []
        for k in range(1, nz):
            gather[s][0][k - 1].wait_recv()
            block = rows_of(lax.rem(z + nz - k, nz) * 2 + core, tb)
            c = remote(t_buf.at[s, block, :], t_buf.at[s, block, :], fw_send.at[s, k], fw_recv.at[s, k], sibling)
            c.start()
            mine_now.append(c)
        pltpu.make_async_copy(sources[s], t_buf.at[s, mine, :], loc_sem.at[s]).wait()
        gather[s][1].wait_recv()
        for c in mine_now:
            c.wait_recv()
        forwards.extend(mine_now)

    def up_cols(j):
        return w_up.at[:, cols_of(j, chunk)], w_col

    def up_rows(j):
        return w_up.at[rows_of(j, chunk), :], w_row

    def down_cols(j):
        return w_down.at[:, cols_of(j, chunk)], w_col

    def down_rows(j):
        return w_down.at[rows_of(j, chunk), :], w_row

    def products(steps, weight, flip, left, target, after):
        def load(j):
            src, buf = weight(j)
            slot = lax.rem(j, 2)
            return pltpu.make_async_copy(src, buf.at[slot], w_sem.at[slot])

        load(0).start()

        def step(j, _):
            @pl.when(j + 1 < steps)
            def _():
                load(j + 1).start()

            load(j).wait()
            block = (w_row if flip else w_col)[lax.rem(j, 2)]
            dims = (((1,), (1 if flip else 0,)), ((), ()))
            got = lax.dot_general(left[...], block, dims, preferred_element_type=F32)
            target[:, cols_of(j, chunk)] = got.astype(BF)
            after(j)
            return 0

        lax.fori_loop(0, steps, step, 0)

    steps = ff // chunk
    per = steps // groups
    gw = per * chunk

    def send_sum(s):
        def after(j):
            g = j // per
            for k in range(1, nr):
                where = rows_of(rpeer(k), rb)
                remote(p_buf.at[s, where, cols_of(j, chunk)], r_buf.at[s, k - 1, :, cols_of(j, chunk)],
                       rs_send.at[s, k], rs_recv.at[s, g, k], (rpeer(k), col)).start()
        return after

    own_rows = rows_of(row, rb)

    def total(s, g):
        cols = cols_of(g, gw)
        for k in range(1, nr):
            view = r_buf.at[s, k - 1, :, cols]
            remote(view, view, rs_send.at[s, k], rs_recv.at[s, g, k], (rpeer(k), col)).wait_recv()
        value = p_buf[s, own_rows, cols].astype(F32)
        for k in range(1, nr):
            value += r_buf[s, k - 1, :, cols].astype(F32)
        return value

    def share(s, g):
        cols = cols_of(g, gw)
        for k in range(1, nr):
            view = g_buf.at[s, own_rows, cols]
            remote(view, view, rg_send.at[s, k], rg_recv.at[s, k], (rpeer(k), col)).start()

    def activate_b(g, _):
        g_buf[0, own_rows, cols_of(g, gw)] = gelu(total(0, g)).astype(BF)
        share(0, g)
        return 0

    def activate_a(g, _):
        value, slope = gelu_both(total(1, g))
        g_buf[1, own_rows, cols_of(g, gw)] = value.astype(BF)
        g_buf[2, own_rows, cols_of(g, gw)] = (total(2, g) * slope).astype(BF)
        share(2, g)
        return 0

    def share_a(g, _):
        share(1, g)
        return 0

    def shared(s):
        for k in range(1, nr):
            view = g_buf.at[s, rows_of(lax.rem(row + nr - k, nr), rb), :]
            remote(view, view, rg_send.at[s, k], rg_recv.at[s, k], (rpeer(k), col)).wait_recv()

    osteps = width // chunk
    oper = osteps // groups
    ow = oper * chunk

    def send_sibling(o):
        def after(j):
            g = j // oper
            for k in range(nz):
                where = rows_of(k * 2 + 1 - core, tb)
                remote(o_buf.at[o, where, cols_of(j, chunk)], sib_buf.at[o, k, :, cols_of(j, chunk)],
                       sb_send.at[o], sb_recv.at[o, g], sibling).start()
        return after

    def combine(o):
        def step(g, _):
            cols = cols_of(g, ow)
            view = sib_buf.at[o, :, :, cols]
            remote(view, view, sb_send.at[o], sb_recv.at[o, g], sibling).wait_recv()
            for k in range(nz):
                where = rows_of(zpeer(k) * 2 + core, tb)
                both = o_buf[o, where, cols].astype(F32) + sib_buf[o, zpeer(k), :, cols].astype(F32)
                o_buf[o, where, cols] = both.astype(BF)
                if k > 0:
                    remote(o_buf.at[o, where, cols], z_buf.at[o, k - 1, :, cols], zs_send.at[o, k],
                           zs_recv.at[o, g, k], (row, zpeer(k) * 2 + core)).start()
            return 0

        lax.fori_loop(0, groups, step, 0)

    def finish(o, target):
        def step(g, _):
            cols = cols_of(g, ow)
            value = o_buf[o, mine, cols].astype(F32)
            for k in range(1, nz):
                view = z_buf.at[o, k - 1, :, cols]
                remote(view, view, zs_send.at[o, k], zs_recv.at[o, g, k], (row, zpeer(k) * 2 + core)).wait_recv()
                value += z_buf[o, k - 1, :, cols].astype(F32)
            target[:, cols] = value.astype(BF)
            return 0

        lax.fori_loop(0, groups, step, 0)

    arrive(0)
    products(steps, up_cols, False, t_buf.at[0], p_buf.at[0], send_sum(0))
    arrive(1)
    products(steps, up_cols, False, t_buf.at[1], p_buf.at[1], send_sum(1))
    lax.fori_loop(0, groups, activate_b, 0)
    arrive(2)
    products(steps, down_rows, True, t_buf.at[2], p_buf.at[2], send_sum(2))
    kept = [
        pltpu.make_async_copy(t_buf.at[1], all_a, out_sem.at[0]),
        pltpu.make_async_copy(t_buf.at[2], all_u, out_sem.at[1]),
    ]
    kept[0].start()
    kept[1].start()
    shared(0)
    products(osteps, down_cols, False, g_buf.at[0], o_buf.at[0], send_sibling(0))
    combine(0)
    lax.fori_loop(0, groups, activate_a, 0)
    lax.fori_loop(0, groups, share_a, 0)
    shared(2)
    products(osteps, up_rows, True, g_buf.at[2], o_buf.at[1], send_sibling(1))
    combine(1)
    kept.append(pltpu.make_async_copy(g_buf.at[2], all_gp, out_sem.at[2]))
    kept[2].start()
    finish(0, out_b)
    shared(1)
    kept.append(pltpu.make_async_copy(g_buf.at[1], all_ga, out_sem.at[3]))
    kept[3].start()
    finish(1, in_grad)

    for c in kept:
        c.wait()
    for s in range(3):
        for c in gather[s][0]:
            c.wait_send()
        gather[s][1].wait_send()
    for c in forwards:
        c.wait_send()
    for s in range(3):
        for k in range(1, nr):
            view = p_buf.at[s, rows_of(rpeer(k), rb), :]
            remote(view, view, rs_send.at[s, k], rg_recv.at[s, k], (rpeer(k), col)).wait_send()
            view = g_buf.at[s, own_rows, :]
            remote(view, view, rg_send.at[s, k], rg_recv.at[s, k], (rpeer(k), col)).wait_send()
    for o in range(2):
        view = sib_buf.at[o]
        remote(view, view, sb_send.at[o], sb_recv.at[o, 0], sibling).wait_send()
        for k in range(1, nz):
            view = o_buf.at[o, rows_of(zpeer(k) * 2 + core, tb), :]
            remote(view, view, zs_send.at[o, k], zs_recv.at[o, 0, k], (row, zpeer(k) * 2 + core)).wait_send()


def exchange(nr, nc, tokens_b, tokens_a, upstream_a, up_weight, down_weight):
    tb, width = tokens_b.shape
    ff = up_weight.shape[1]
    tokens = tb * nc
    rb = tokens // nr
    nz = nc // 2
    chunk = 256
    groups = next(g for g in (4, 3, 2, 1) if (ff // chunk) % g == 0 and (width // chunk) % g == 0)
    dma = pltpu.SemaphoreType.DMA
    anywhere = pl.BlockSpec(memory_space=pl.ANY)
    near = pl.BlockSpec(memory_space=pltpu.VMEM)
    whole = jax.ShapeDtypeStruct((tokens, width), BF)
    hidden = jax.ShapeDtypeStruct((tokens, ff), BF)
    block = jax.ShapeDtypeStruct((tb, width), BF)
    return pl.pallas_call(
        functools.partial(kernel, nr, nc, chunk, groups),
        out_shape=(block, block, whole, whole, hidden, hidden),
        in_specs=[anywhere] * 5,
        out_specs=(near, near, anywhere, anywhere, anywhere, anywhere),
        scratch_shapes=[
            pltpu.VMEM((3, tokens, width), BF),
            pltpu.VMEM((3, tokens, ff), BF),
            pltpu.VMEM((3, nr - 1, rb, ff), BF),
            pltpu.VMEM((3, tokens, ff), BF),
            pltpu.VMEM((2, tokens, width), BF),
            pltpu.VMEM((2, nz, tb, width), BF),
            pltpu.VMEM((2, nz - 1, tb, width), BF),
            pltpu.VMEM((2, max(width, ff), chunk), BF),
            pltpu.VMEM((2, chunk, max(width, ff)), BF),
            dma((3, nz)), dma((3, nz)), dma((3, nz)), dma((3, nz)),
            dma((3, nr)), dma((3, groups, nr)), dma((3, nr)), dma((3, nr)),
            dma((2,)), dma((2, groups)), dma((2, nz)), dma((2, groups, nz)),
            dma((3,)), dma((2,)), dma((4,)),
        ],
        compiler_params=pltpu.CompilerParams(
            collective_id=0, has_side_effects=True, vmem_limit_bytes=62 * 1024 * 1024
        ),
        cost_estimate=pl.CostEstimate(
            flops=10 * tokens * width * ff, bytes_accessed=8 * width * ff, transcendentals=0
        ),
    )(tokens_b, tokens_a, upstream_a, up_weight, down_weight)


def on_device(nr, nc, tokens_b, tokens_a, upstream_a, up_weight, down_weight):
    output_b, input_grad, inputs_a, upstream, gated_a, grad_pre = exchange(
        nr, nc, tokens_b, tokens_a, upstream_a, up_weight, down_weight
    )
    up_grad = lax.dot_general(inputs_a, grad_pre, (((0,), (0,)), ((), ())), preferred_element_type=F32)
    down_grad = lax.dot_general(gated_a, upstream, (((0,), (0,)), ((), ())), preferred_element_type=F32)
    return output_b, input_grad, up_grad.astype(BF), down_grad.astype(BF)


def solution(mesh):
    placed = (P("col", "row"), P("col", "row"), P("col", "row"), P("row", "col"), P("col", "row"))
    return jax.shard_map(
        functools.partial(on_device, mesh.shape["row"], mesh.shape["col"]),
        mesh=mesh,
        in_specs=placed,
        out_specs=(P("col", "row"), P("col", "row"), P("row", "col"), P("col", "row")),
        check_vma=False,
    )
```

time: 500 us -> 313 us (0.63)
  waiting for transfers between devices: 340 us -> 0 us
  Pallas kernels: 0 us -> 280 us
  matrix products: 109 us -> 30 us
  local copies, waits for them, and re-layouts: 26.6 us -> 1.51 us
  between operations: 13.9 us -> 0.67 us
  other arithmetic: 6.29 us -> 0 us
    pallas_call x0 -> x1, Pallas kernels: none -> 280 us  [exchange(): pl.pallas_call(functools.partial(kernel, nr, nc, chunk, groups), out_shap...]
    reduce_scatter x5 -> x0, waiting for transfers between devices: 181 us -> none  [the longest x1 47.4 us: on_device(): lax.psum_scatter(partial_a.astype(jnp.bfloat16), 'row', scatter_dimension...]
    all_gather x6 -> x0, waiting for transfers between devices: 156 us -> none  [the longest x1 41.9 us: on_device(): lax.all_gather(share_b, 'row', axis=0, tiled=True)]
    dot_general x5 -> x0, matrix products: 79.3 us -> none  [the longest x1 15.9 us: on_device(): lax.dot_general(grad_pre, up_weight, (((1,), (1,)), ((), ())), preferred_...]
    unnamed x5 -> x10, local copies, waits for them, and re-layouts: 26.6 us -> 1.51 us
    convert_element_type x2 -> x0, other arithmetic: 6.29 us -> none  [the longest x1 3.74 us: activate(): return (gated_b, gated_full.astype(jnp.bfloat16), grad_pre)]
  transfers between devices with their start and end apart: 11 -> 0, of which waited for: 10 -> 0; matrix products, arithmetic and copies ran while one was open for 28% -> 0% of each run, Pallas kernels for 0% -> 0%
where the time goes in v1:
time: 313 us; the launch traced here: 312 us
  Pallas kernels  280 us (89%)
  matrix products  30 us (10%)
    pallas_call x1, Pallas kernels, exchange(): pl.pallas_call(functools.partial(kernel, nr, nc, chunk, groups), out_shap...  280 us
    dot_general x1, matrix products, on_device(): lax.dot_general(inputs_a, grad_pre, (((0,), (0,)), ((), ())), preferred_e...  16.5 us
    dot_general x1, matrix products, on_device(): lax.dot_general(gated_a, upstream, (((0,), (0,)), ((), ())), preferred_el...  13.5 us

profile of v1, /device:TPU:29, one launch (start us, length us, event | category | flops | bytes accessed | tf_op | source)
XLA Modules:
  0.0 312.0 jit_solution(18286896446249321165)
XLA Ops:
  0.6 279.8 %shard_map.84 = (bf16[64,3072]{1,0:T(8,128)(2,1)}, bf16[64,3072]{1,0:T(8,128)(2,1)}, bf16[512,3072]{1,0:T(8,128)(2,1)}, bf16[512,3072]{1,0:T(8,128)(2,1)}, bf16[...) custom-call(bf16[64,3072]{1,0:T(8,128)(2,1)} %tok_b.1, bf16[64,3072]{1,0:T(8,128)(2,1)} %tok_a.1, bf16[64,3072]{1,0:T(8,128)(2,1)} %ups.1, ...), custom_call_target="tpu_custom_call" | custom-call | flops 48318382080 | bytes 75497472 | tf_op jit(solution)/shard_map/pallas_call | solution.py:297
  280.5 0.0 copy-start.2
  280.5 0.0 copy-start.3
  280.5 16.5 %convolution_convert_fusion.1 = bf16[3072,3072]{1,0:T(8,128)(2,1)} fusion(bf16[512,3072]{1,0:T(8,128)(2,1)} %get-tuple-element.12, bf16[512,3072]{1,0:T(8,128)(2,1)} %get-tuple-element.13), kind=kOutput, calls=%fused_computation.1 | convolution fusion | flops 9673113600 | bytes 25165824 | tf_op jit(solution)/shard_map/dot_general | solution.py:330
  297.0 0.0 copy-done.2
  297.0 0.0 copy-done.3
  297.0 0.0 copy-start.1
  297.0 0.0 copy-start
  297.0 13.5 %convolution_convert_fusion = bf16[3072,3072]{1,0:T(8,128)(2,1)} fusion(bf16[512,3072]{1,0:T(8,128)(2,1)S(1)} %copy-done.3, bf16[512,3072]{1,0:T(8,128)(2,1)S(1)} %copy-done.2), kind=kOutput, calls=%fused_computation | convolution fusion | flops 9673113600 | bytes 25165824 | tf_op jit(solution)/shard_map/dot_general | solution.py:331
  310.5 0.0 copy-done.1
  310.5 0.7 copy.11
  311.3 0.0 copy-done
  311.3 0.7 copy.12
Async XLA Ops:
  280.5 16.5 %copy-start.2 = (bf16[512,3072]{1,0:T(8,128)(2,1)S(1)}, bf16[512,3072]{1,0:T(8,128)(2,1)}, u32[]{:S(2)}) copy-start(bf16[512,3072]{1,0:T(8,128)(2,1)} %get-tuple-element.15) | copy-start | bytes 9437188
  280.5 16.5 %copy-start.3 = (bf16[512,3072]{1,0:T(8,128)(2,1)S(1)}, bf16[512,3072]{1,0:T(8,128)(2,1)}, u32[]{:S(2)}) copy-start(bf16[512,3072]{1,0:T(8,128)(2,1)} %get-tuple-element.14) | copy-start | bytes 9437188
  297.0 13.5 %copy-start.1 = (bf16[64,3072]{1,0:T(8,128)(2,1)S(1)}, bf16[64,3072]{1,0:T(8,128)(2,1)}, u32[]{:S(2)}) copy-start(bf16[64,3072]{1,0:T(8,128)(2,1)} %get-tuple-element.20) | copy-start | bytes 1179652
  297.0 14.3 %copy-start = (bf16[64,3072]{1,0:T(8,128)(2,1)S(1)}, bf16[64,3072]{1,0:T(8,128)(2,1)}, u32[]{:S(2)}) copy-start(bf16[64,3072]{1,0:T(8,128)(2,1)} %get-tuple-element.21) | copy-start | bytes 1179652

commit v2 on v1

--- a/solution.py
+++ b/solution.py
@@ -198,23 +198,23 @@
                 where = rows_of(k * 2 + 1 - core, tb)
                 remote(o_buf.at[o, where, cols_of(j, chunk)], sib_buf.at[o, k, :, cols_of(j, chunk)],
                        sb_send.at[o], sb_recv.at[o, g], sibling).start()
+
+            @pl.when(jnp.logical_and(lax.rem(j, oper) == oper - 1, g > 0))
+            def _():
+                combine(o, g - 1)
         return after
 
-    def combine(o):
-        def step(g, _):
-            cols = cols_of(g, ow)
-            view = sib_buf.at[o, :, :, cols]
-            remote(view, view, sb_send.at[o], sb_recv.at[o, g], sibling).wait_recv()
-            for k in range(nz):
-                where = rows_of(zpeer(k) * 2 + core, tb)
-                both = o_buf[o, where, cols].astype(F32) + sib_buf[o, zpeer(k), :, cols].astype(F32)
-                o_buf[o, where, cols] = both.astype(BF)
-                if k > 0:
-                    remote(o_buf.at[o, where, cols], z_buf.at[o, k - 1, :, cols], zs_send.at[o, k],
-                           zs_recv.at[o, g, k], (row, zpeer(k) * 2 + core)).start()
-            return 0
-
-        lax.fori_loop(0, groups, step, 0)
+    def combine(o, g):
+        cols = cols_of(g, ow)
+        view = sib_buf.at[o, :, :, cols]
+        remote(view, view, sb_send.at[o], sb_recv.at[o, g], sibling).wait_recv()
+        for k in range(nz):
+            where = rows_of(zpeer(k) * 2 + core, tb)
+            both = o_buf[o, where, cols].astype(F32) + sib_buf[o, zpeer(k), :, cols].astype(F32)
+            o_buf[o, where, cols] = both.astype(BF)
+            if k > 0:
+                remote(o_buf.at[o, where, cols], z_buf.at[o, k - 1, :, cols], zs_send.at[o, k],
+                       zs_recv.at[o, g, k], (row, zpeer(k) * 2 + core)).start()
 
     def finish(o, target):
         def step(g, _):
@@ -242,14 +242,14 @@
     ]
     kept[0].start()
     kept[1].start()
+    lax.fori_loop(0, groups, activate_a, 0)
+    lax.fori_loop(0, groups, share_a, 0)
     shared(0)
     products(osteps, down_cols, False, g_buf.at[0], o_buf.at[0], send_sibling(0))
-    combine(0)
-    lax.fori_loop(0, groups, activate_a, 0)
-    lax.fori_loop(0, groups, share_a, 0)
+    combine(0, groups - 1)
     shared(2)
     products(osteps, up_rows, True, g_buf.at[2], o_buf.at[1], send_sibling(1))
-    combine(1)
+    combine(1, groups - 1)
     kept.append(pltpu.make_async_copy(g_buf.at[2], all_gp, out_sem.at[2]))
     kept[2].start()
     finish(0, out_b)
@@ -287,7 +287,7 @@
     rb = tokens // nr
     nz = nc // 2
     chunk = 256
-    groups = next(g for g in (4, 3, 2, 1) if (ff // chunk) % g == 0 and (width // chunk) % g == 0)
+    groups = next(g for g in (6, 4, 3, 2, 1) if (ff // chunk) % g == 0 and (width // chunk) % g == 0)
     dma = pltpu.SemaphoreType.DMA
     anywhere = pl.BlockSpec(memory_space=pl.ANY)
     near = pl.BlockSpec(memory_space=pltpu.VMEM)

time: 313 us -> 305 us (0.974)
  Pallas kernels: 280 us -> 271 us
    pallas_call x1, Pallas kernels: 280 us -> 271 us  [exchange(): pl.pallas_call(functools.partial(kernel, nr, nc, chunk, groups), out_shap...]
where the time goes in v2:
time: 305 us; the launch traced here: 304 us
  Pallas kernels  271 us (89%)
  matrix products  30 us (10%)
    pallas_call x1, Pallas kernels, exchange(): pl.pallas_call(functools.partial(kernel, nr, nc, chunk, groups), out_shap...  271 us
    dot_general x1, matrix products, on_device(): lax.dot_general(inputs_a, grad_pre, (((0,), (0,)), ((), ())), preferred_e...  16.5 us
    dot_general x1, matrix products, on_device(): lax.dot_general(gated_a, upstream, (((0,), (0,)), ((), ())), preferred_el...  13.5 us

profile of v2, /device:TPU:29, one launch (start us, length us, event | category | flops | bytes accessed | tf_op | source)
XLA Modules:
  0.0 303.6 jit_solution(230856452815820322)
XLA Ops:
  0.6 271.4 %shard_map.84 = (bf16[64,3072]{1,0:T(8,128)(2,1)}, bf16[64,3072]{1,0:T(8,128)(2,1)}, bf16[512,3072]{1,0:T(8,128)(2,1)}, bf16[512,3072]{1,0:T(8,128)(2,1)}, bf16[...) custom-call(bf16[64,3072]{1,0:T(8,128)(2,1)} %tok_b.1, bf16[64,3072]{1,0:T(8,128)(2,1)} %tok_a.1, bf16[64,3072]{1,0:T(8,128)(2,1)} %ups.1, ...), custom_call_target="tpu_custom_call" | custom-call | flops 48318382080 | bytes 75497472 | tf_op jit(solution)/shard_map/pallas_call | solution.py:297
  272.0 0.0 copy-start.2
  272.0 0.0 copy-start.3
  272.0 16.5 %convolution_convert_fusion.1 = bf16[3072,3072]{1,0:T(8,128)(2,1)} fusion(bf16[512,3072]{1,0:T(8,128)(2,1)} %get-tuple-element.12, bf16[512,3072]{1,0:T(8,128)(2,1)} %get-tuple-element.13), kind=kOutput, calls=%fused_computation.1 | convolution fusion | flops 9673113600 | bytes 25165824 | tf_op jit(solution)/shard_map/dot_general | solution.py:330
  288.5 0.0 copy-done.2
  288.5 0.0 copy-done.3
  288.5 0.0 copy-start.1
  288.5 0.0 copy-start
  288.6 13.5 %convolution_convert_fusion = bf16[3072,3072]{1,0:T(8,128)(2,1)} fusion(bf16[512,3072]{1,0:T(8,128)(2,1)S(1)} %copy-done.3, bf16[512,3072]{1,0:T(8,128)(2,1)S(1)} %copy-done.2), kind=kOutput, calls=%fused_computation | convolution fusion | flops 9673113600 | bytes 25165824 | tf_op jit(solution)/shard_map/dot_general | solution.py:331
  302.1 0.0 copy-done.1
  302.1 0.7 copy.11
  302.8 0.0 copy-done
  302.8 0.7 copy.12
Async XLA Ops:
  272.0 16.5 %copy-start.2 = (bf16[512,3072]{1,0:T(8,128)(2,1)S(1)}, bf16[512,3072]{1,0:T(8,128)(2,1)}, u32[]{:S(2)}) copy-start(bf16[512,3072]{1,0:T(8,128)(2,1)} %get-tuple-element.15) | copy-start | bytes 9437188
  272.0 16.5 %copy-start.3 = (bf16[512,3072]{1,0:T(8,128)(2,1)S(1)}, bf16[512,3072]{1,0:T(8,128)(2,1)}, u32[]{:S(2)}) copy-start(bf16[512,3072]{1,0:T(8,128)(2,1)} %get-tuple-element.14) | copy-start | bytes 9437188
  288.5 13.5 %copy-start.1 = (bf16[64,3072]{1,0:T(8,128)(2,1)S(1)}, bf16[64,3072]{1,0:T(8,128)(2,1)}, u32[]{:S(2)}) copy-start(bf16[64,3072]{1,0:T(8,128)(2,1)} %get-tuple-element.20) | copy-start | bytes 1179652
  288.5 14.3 %copy-start = (bf16[64,3072]{1,0:T(8,128)(2,1)S(1)}, bf16[64,3072]{1,0:T(8,128)(2,1)}, u32[]{:S(2)}) copy-start(bf16[64,3072]{1,0:T(8,128)(2,1)} %get-tuple-element.21) | copy-start | bytes 1179652
